TPU v7x, 128 devices: a whole 4x4x4 slice. The times are simulated.
128 devices in a mesh: loader: 32 (over x, y, core), pack: 4 (over z).
Axes of the slice: x: 4, y: 4, z: 4, core: 2. Of those that a mesh axis runs over, the one named last changes fastest.
Arguments:
- patches: bfloat16 [49152, 11, 256], P(('loader', 'pack')), may hold values from -6 to 6
- fields: int32 [49152], P(('loader', 'pack')), may hold values from 4 to 11, as said below
- route: int32 [49152], P(('loader', 'pack')), may hold values from 0 to 127, as said below
- frame: int32 [49152], P(('loader', 'pack')), may hold values from 0 to 3, as said below
- embed: bfloat16 [11, 256, 1024], replicated, may hold values from -0.109375 to 0.109375
- norm_attn: float32 [1024], replicated, may hold values from 0.5 to 1.5
- attn_in: bfloat16 [1024, 3072], P(None, 'pack')
- attn_out: bfloat16 [1024, 1024], P('pack'), may hold values from -0.1875 to 0.1875
- norm_mlp: float32 [1024], replicated, may hold values from 0.5 to 1.5
- mlp_in: bfloat16 [1024, 4096], P(None, 'pack'), may hold values from -0.1875 to 0.1875
- mlp_out: bfloat16 [4096, 1024], P('pack'), may hold values from -0.09375 to 0.09375
Outputs:
- mixed: bfloat16 [49152, 1024], P(('loader', 'pack'))
Inputs may be any that keep to these rules, and one draw needn't show every extreme that they name: `route`: every device sends all its 384 tokens, at most 6 of them to one owner. Some owner receives exactly 6 tokens from every device, so 768 live slots; some owner receives none; the others receive from 0 to 6 from each device. Tokens attend only to tokens with the same owner and frame. `fields`: equal for all tokens with the same owner and frame.
All inputs are finite; a program needn't handle non-finite values.
Results may differ from a plain program's by a relative error of at most 0.01.
Values may be sent and summed in bfloat16 or wider, within the bound.
A program may use at most 128 MiB of HBM per device.

v0:
```python
import jax
import jax.numpy as jnp
from jax import lax
from jax.sharding import PartitionSpec as P

D = 1024
HEADS = 16
HEAD_WIDTH = 64
FIELDS = 11
PATCH = 256


def rms_norm(values, gain):
    mean_square = jnp.mean(values * values, axis=-1, keepdims=True)
    return values * lax.rsqrt(mean_square + 1e-06) * gain


def attend(qkv, tags):
    same = tags[:, :, None] == tags[:, None, :]
    heads = jnp.moveaxis(qkv, 2, 0)

    def one_head(part):
        query_rows = part[:, :, 0]
        key_rows = part[:, :, 1]
        value_rows = part[:, :, 2]
        logit_scores = jnp.einsum(
            "ecl,enl->ecn", query_rows, key_rows, preferred_element_type=jnp.float32
        ) * HEAD_WIDTH ** (-0.5)
        logit_scores = jnp.where(same, logit_scores, -1e30)
        highest = jnp.max(logit_scores, axis=-1, keepdims=True)
        shifted = jnp.exp(logit_scores - highest)
        attention_weight = (shifted / jnp.sum(shifted, axis=-1, keepdims=True)).astype(jnp.bfloat16)
        return jnp.einsum(
            "ivn,inf->ivf", attention_weight, value_rows, preferred_element_type=jnp.float32
        ).astype(jnp.bfloat16)

    result = lax.map(one_head, heads)
    result = jnp.moveaxis(result, 0, 2)
    return result.reshape(result.shape[0], result.shape[1], -1)


def local(
    patches, fields, route, frame, embed, norm_attn, attn_in, attn_out, norm_mlp, mlp_in, mlp_out
):
    row_count = patches.shape[0]
    loaders = lax.axis_size("loader")
    packers = lax.axis_size("pack")
    owners = loaders * packers
    most = 2 * row_count // owners
    slots = owners * most
    live = jnp.arange(FIELDS, dtype=jnp.int32)[None, :] < fields[:, None]
    flat = jnp.where(live[:, :, None], patches, jnp.zeros_like(patches)).reshape(
        row_count, FIELDS * PATCH
    )
    embedded = jnp.dot(
        flat, embed.reshape(FIELDS * PATCH, D), preferred_element_type=jnp.float32
    ).astype(jnp.bfloat16)
    onehot = (route[:, None] == jnp.arange(owners, dtype=jnp.int32)[None, :]).astype(jnp.int32)
    rank = jnp.sum((jnp.cumsum(onehot, axis=0) - onehot) * onehot, axis=1)
    target = route * most + rank
    outgoing = jnp.zeros((slots, D), jnp.bfloat16).at[target].set(embedded)
    labels = jnp.full((slots,), -1.0, jnp.bfloat16).at[target].set(frame.astype(jnp.bfloat16))
    arrived, arrived_tags = (
        lax.all_to_all(
            outgoing.reshape(owners, most, D),
            ("loader", "pack"),
            split_axis=0,
            concat_axis=0,
            tiled=True,
        ),
        lax.all_to_all(
            labels.reshape(owners, most),
            ("loader", "pack"),
            split_axis=0,
            concat_axis=0,
            tiled=True,
        ),
    )
    owner_rows = arrived.reshape(slots, D)
    owner_tags = arrived_tags.reshape(slots)
    residual = owner_rows.astype(jnp.float32)
    normed = rms_norm(residual, norm_attn).astype(jnp.bfloat16)
    whole_in, whole_out, whole_up, whole_down = (
        lax.all_gather(attn_in, "pack", axis=1, tiled=True),
        lax.all_gather(attn_out, "pack", axis=0, tiled=True),
        lax.all_gather(mlp_in, "pack", axis=1, tiled=True),
        lax.all_gather(mlp_out, "pack", axis=0, tiled=True),
    )
    qkv = jnp.dot(normed, whole_in, preferred_element_type=jnp.float32).astype(jnp.bfloat16)
    qkv = qkv.reshape(1, slots, HEADS, 3, HEAD_WIDTH)
    heads_out = attend(qkv, owner_tags.astype(jnp.int32)[None, :])[0]
    hidden_state = residual + jnp.dot(heads_out, whole_out, preferred_element_type=jnp.float32)
    normed_mlp = rms_norm(hidden_state, norm_mlp).astype(jnp.bfloat16)
    inner = jax.nn.gelu(jnp.dot(normed_mlp, whole_up, preferred_element_type=jnp.float32)).astype(
        jnp.bfloat16
    )
    layer_out = (
        hidden_state + jnp.dot(inner, whole_down, preferred_element_type=jnp.float32)
    ).astype(jnp.bfloat16)
    returned = lax.all_to_all(
        layer_out.reshape(owners, most, D),
        ("loader", "pack"),
        split_axis=0,
        concat_axis=0,
        tiled=True,
    )
    return returned.reshape(slots, D)[target]


def solution(mesh):
    return jax.shard_map(
        local,
        mesh=mesh,
        in_specs=(
            P(("loader", "pack"), None, None),
            P(("loader", "pack")),
            P(("loader", "pack")),
            P(("loader", "pack")),
            P(),
            P(),
            P(None, "pack"),
            P("pack", None),
            P(),
            P(None, "pack"),
            P("pack", None),
        ),
        out_specs=P(("loader", "pack"), None),
        check_vma=False,
    )
```

profile of v0, /device:TPU:1, one launch (start us, length us, event | category | flops | bytes accessed | tf_op | source)
XLA Modules:
  0.0 379.5 jit_solution(9187672909685559910)
XLA Ops:
  9.5 3.0 scatter_custom_fusion.1
  13.2 11.5 %all-to-all-start.1 = ((bf16[128,1,6]{2,1,0:T(2,128)(2,1)}), bf16[128,1,6]{2,1,0:T(2,128)(2,1)S(1)}, u32[]{:S(2)}, u32[]{:S(2)}) async-start(bf16[128,1,6]{2,1,0:T(2,128)(2,1)} %all_to_all.16), calls=%async_computation.1 | async-start | bytes 131072 | tf_op jit(solution)/shard_map/all_to_all | solution.py:71
  24.8 6.2 %bitcast_convert_fusion = bf16[384,1024]{1,0:T(8,128)(2,1)S(1)} fusion(bf16[11,256,1024]{2,1,0:T(8,128)(2,1)} %param.17, bf16[384,11,256]{2,0,1:T(8,128)(2,1)} %param.13, pred[384,11]{0,1:T(8,128)(4,1)S(1)} %iota_compare_fusion.3), kind=kOutput, calls=%fused_computation.37 | convolution fusion | flops 2216067072 | bytes 8720512 | tf_op jit(solution)/shard_map/dot_general | solution.py:55
  31.0 2.6 scatter_custom_fusion
  33.6 1.6 reshape.186
  35.2 9.7 %all-to-all-start = ((bf16[128,6,1024]{2,1,0:T(8,128)(2,1)}), bf16[128,6,1024]{2,1,0:T(8,128)(2,1)S(1)}, u32[]{:S(2)}, u32[]{:S(2)}) async-start(bf16[128,6,1024]{2,1,0:T(8,128)(2,1)} %reshape.186), calls=%async_computation | async-start | bytes 4194304 | tf_op jit(solution)/shard_map/all_to_all | solution.py:64
  45.8 30.0 %all-to-all-done = bf16[128,6,1024]{2,1,0:T(8,128)(2,1)S(1)} async-done(((bf16[128,6,1024]{2,1,0:T(8,128)(2,1)}), bf16[128,6,1024]{2,1,0:T(8,128)(2,1)S(1)}, u32[]{:S(2)}, u32[]{:S(2)}) %all-to-all-start) | async-done | bytes 1572896 | tf_op jit(solution)/shard_map/all_to_all | solution.py:64
  76.6 2.0 reshape.190
  78.5 22.8 %all-gather.5.cloned.1.call-done = bf16[1024,3072]{1,0:T(8,128)(2,1)} async-done(((bf16[1024,768]{1,0:T(8,128)(2,1)}), bf16[1024,3072]{1,0:T(8,128)(2,1)}) %all-gather.5.cloned.1.call-update) | async-done | bytes 6291472 | tf_op jit(solution)/shard_map/all_gather | solution.py:84
  101.3 9.8 %convolution_convert_fusion = bf16[768,3072]{1,0:T(8,128)(2,1)} fusion(bf16[1024,3072]{1,0:T(8,128)(2,1)} %all-gather.5.cloned.1.call-done, f32[768,1024]{1,0:T(8,128)} %reshape.190, f32[1024]{0:T(1024)S(1)} %copy-done.4, f32[768]{0:T(1024)S(1)} %rsqrt.20), kind=kOutput, calls=%fused_computation.26 | convolution fusion | flops 4836556800 | bytes 14162944 | tf_op jit(solution)/shard_map/dot_general | solution.py:89
  111.1 6.6 %copy.19 = bf16[768,3072]{0,1:T(8,128)(2,1)} copy(bf16[768,3072]{1,0:T(8,128)(2,1)} %convolution_convert_fusion) | data formatting | bytes 9437184 | tf_op jit(solution)/shard_map/convert_element_type | solution.py:89
  117.7 49.1 %while.11 = (s32[]{:T(128)}, bf16[16,1,768,64]{2,3,1,0:T(8,128)(2,1)}, bf16[16,1,768,3,64]{2,4,3,1,0:T(8,128)(2,1)}, s32[768]{0:T(1024)S(1)}, s32[]{:T(128)}) while((s32[]{:T(128)}, bf16[16,1,768,64]{2,3,1,0:T(8,128)(2,1)}, bf16[16,1,768,3,64]{2,4,3,1,0:T(8,128)(2,1)}, s32[768]{0:T(1024)S(1)}, s32[]{:T(128)}) %tuple.38), condition=%wide.region_9.10_spmd.clone, body=%wide.region_6.9_spmd.clone.sunk | while | flops 156350976 | bytes 8087105 | solution.py:37
  117.7 1.1 dynamic-slice_bitcast_fusion.2
  119.8 1.1 fusion.58
  120.9 1.0 dynamic-slice_bitcast_fusion.2
  122.8 1.2 fusion.58
  124.0 1.0 dynamic-slice_bitcast_fusion.2
  125.9 1.2 fusion.58
  127.1 1.0 dynamic-slice_bitcast_fusion.2
  129.0 1.1 fusion.58
  132.0 1.2 fusion.58
  133.2 1.0 dynamic-slice_bitcast_fusion.2
  135.1 1.2 fusion.58
  138.1 1.2 fusion.58
  141.1 1.2 fusion.58
  144.2 1.2 fusion.58
  145.4 1.0 dynamic-slice_bitcast_fusion.2
  147.3 1.1 fusion.58
  148.4 1.0 dynamic-slice_bitcast_fusion.2
  150.4 1.2 fusion.58
  151.5 1.0 dynamic-slice_bitcast_fusion.2
  153.4 1.1 fusion.58
  154.6 1.0 dynamic-slice_bitcast_fusion.2
  156.5 1.2 fusion.58
  157.6 1.0 dynamic-slice_bitcast_fusion.2
  159.5 1.2 fusion.58
  162.6 1.2 fusion.58
  163.8 1.0 dynamic-slice_bitcast_fusion.2
  165.7 1.2 fusion.58
  166.8 5.6 %multiply_reduce_fusion.1 = (f32[768]{0:T(1024)S(1)}, f32[768,1024]{1,0:T(8,128)}) fusion(f32[768,1024]{1,0:T(8,128)S(1)} %copy-done, bf16[768,1024]{0,1:T(8,128)(2,1)} %bitcast.9, bf16[1024,1024]{1,0:T(8,128)(2,1)} %all-gather.7.cloned.1.call-done), kind=kOutput, calls=%fused_computation.30 | convolution fusion | flops 1612971264 | bytes 9964544 | tf_op jit(solution)/shard_map/dot_general | solution.py:92
  172.4 47.1 %all-gather.11.cloned.1.call-done = bf16[4096,1024]{1,0:T(8,128)(2,1)} async-done(((bf16[1024,1024]{1,0:T(8,128)(2,1)}), bf16[4096,1024]{1,0:T(8,128)(2,1)}) %all-gather.11.cloned.1.call-update) | async-done | bytes 8388624 | tf_op jit(solution)/shard_map/all_gather | solution.py:87
  219.5 85.7 %all-gather.9.cloned.1.call-done = bf16[1024,4096]{1,0:T(8,128)(2,1)} async-done(((bf16[1024,1024]{1,0:T(8,128)(2,1)}), bf16[1024,4096]{1,0:T(8,128)(2,1)}) %all-gather.9.cloned.1.call-update) | async-done | bytes 8388624 | tf_op jit(solution)/shard_map/all_gather | solution.py:86
  305.2 20.9 %add_convert_fusion = bf16[768,1024]{1,0:T(8,128)(2,1)S(1)} fusion(f32[768,1024]{1,0:T(8,128)} %get-tuple-element.58, bf16[4096,1024]{1,0:T(8,128)(2,1)} %all-gather.11.cloned.1.call-done, bf16[1024,4096]{1,0:T(8,128)(2,1)} %all-gather.9.cloned.1.call-done, f32[1024]{0:T(1024)S(1)} %copy-done.5, f32[768]{0:T(1024)S(1)} %add_rsqrt_fusion.1), kind=kOutput, calls=%fused_computation.28 | convolution fusion | flops 12917145600 | bytes 21502976 | tf_op jit(solution)/shard_map/dot_general | solution.py:98
  326.1 1.6 reshape.188
  327.7 9.6 %all-to-all-start.2 = ((bf16[128,6,1024]{2,1,0:T(8,128)(2,1)}), bf16[128,6,1024]{2,1,0:T(8,128)(2,1)}, u32[]{:S(2)}, u32[]{:S(2)}) async-start(bf16[128,6,1024]{2,1,0:T(8,128)(2,1)} %reshape.188), calls=%async_computation.2 | async-start | bytes 4194304 | tf_op jit(solution)/shard_map/all_to_all | solution.py:100
  337.3 30.5 %all-to-all-done.2 = bf16[128,6,1024]{2,1,0:T(8,128)(2,1)} async-done(((bf16[128,6,1024]{2,1,0:T(8,128)(2,1)}), bf16[128,6,1024]{2,1,0:T(8,128)(2,1)}, u32[]{:S(2)}, u32[]{:S(2)}) %all-to-all-start.2) | async-done | bytes 1572896 | tf_op jit(solution)/shard_map/all_to_all | solution.py:100
  367.7 2.6 reshape.189
  370.3 2.7 gather_fusion
  (78 shorter events, 24.7 us)
Async XLA Ops:
  6.5 2.2 copy-start.1
  6.5 94.8 %all-gather.5.cloned.1.call-start = ((), (), s32[]{:S(2)}) async-start(), calls=%async_computation.3 | async-start | bytes 7864320 | tf_op jit(solution)/shard_map/all_gather | solution.py:84
  7.3 2.0 copy-start.2
  7.3 17.5 %copy-start.3 = (s32[384]{0:T(512)S(1)}, s32[384]{0:T(512)}, u32[]{:S(2)}) copy-start(s32[384]{0:T(512)} %param.14) | copy-start | bytes 4612
  7.3 159.5 %all-gather.7.cloned.1.call-start = ((), (), s32[]{:S(2)}) async-start(), calls=%async_computation.4 | async-start | bytes 2621440 | tf_op jit(solution)/shard_map/all_gather | solution.py:85
  8.0 211.5 %all-gather.11.cloned.1.call-start = ((), (), s32[]{:S(2)}) async-start(), calls=%async_computation.6 | async-start | bytes 10485760 | tf_op jit(solution)/shard_map/all_gather | solution.py:87
  13.2 22.0 %all-to-all-start.1 = ((bf16[128,1,6]{2,1,0:T(2,128)(2,1)}), bf16[128,1,6]{2,1,0:T(2,128)(2,1)S(1)}, u32[]{:S(2)}, u32[]{:S(2)}) async-start(bf16[128,1,6]{2,1,0:T(2,128)(2,1)} %all_to_all.16), calls=%async_computation.1 | async-start | bytes 131072 | tf_op jit(solution)/shard_map/all_to_all | solution.py:71
  35.2 40.6 %all-to-all-start = ((bf16[128,6,1024]{2,1,0:T(8,128)(2,1)}), bf16[128,6,1024]{2,1,0:T(8,128)(2,1)S(1)}, u32[]{:S(2)}, u32[]{:S(2)}) async-start(bf16[128,6,1024]{2,1,0:T(8,128)(2,1)} %reshape.186), calls=%async_computation | async-start | bytes 4194304 | tf_op jit(solution)/shard_map/all_to_all | solution.py:64
  44.9 260.3 %all-gather.9.cloned.1.call-start = ((), (), s32[]{:S(2)}) async-start(), calls=%async_computation.5 | async-start | bytes 10485760 | tf_op jit(solution)/shard_map/all_gather | solution.py:86
  76.6 24.8 %copy-start.4 = (f32[1024]{0:T(1024)S(1)}, f32[1024]{0:T(1024)}, u32[]{:S(2)}) copy-start(f32[1024]{0:T(1024)} %param.18) | copy-start | bytes 12292
  117.7 49.1 %copy-start = (f32[768,1024]{1,0:T(8,128)S(1)}, f32[768,1024]{1,0:T(8,128)}, u32[]{:S(2)}) copy-start(f32[768,1024]{1,0:T(8,128)} %reshape.190) | copy-start | bytes 9437188
  166.8 138.4 %copy-start.5 = (f32[1024]{0:T(1024)S(1)}, f32[1024]{0:T(1024)}, u32[]{:S(2)}) copy-start(f32[1024]{0:T(1024)} %param.21) | copy-start | bytes 12292
  327.7 40.1 %all-to-all-start.2 = ((bf16[128,6,1024]{2,1,0:T(8,128)(2,1)}), bf16[128,6,1024]{2,1,0:T(8,128)(2,1)}, u32[]{:S(2)}, u32[]{:S(2)}) async-start(bf16[128,6,1024]{2,1,0:T(8,128)(2,1)} %reshape.188), calls=%async_computation.2 | async-start | bytes 4194304 | tf_op jit(solution)/shard_map/all_to_all | solution.py:100
Sparse Core Ops, SparseCore 0:
  9.0 92.2 all-gather.4
  103.0 31.5 all-gather.6
  136.3 83.1 all-gather.10
  221.0 84.1 all-gather.8
where the time goes:
time: 381 us; the launch traced here: 380 us
  waiting for transfers between devices  218 us (57%)
  matrix products  69.5 us (18%)
  local copies, waits for them, and re-layouts  39.8 us (10%)
  starting transfers between devices  31 us (8%)
  between operations  13.3 us (3%)
  other arithmetic  7.3 us (2%)
    all_gather x1, waiting for transfers between devices, local(): lax.all_gather(mlp_in, 'pack', axis=1, tiled=True)  85.7 us
    all_gather x1, waiting for transfers between devices, local(): lax.all_gather(mlp_out, 'pack', axis=0, tiled=True)  47.1 us
    all_to_all x1, waiting for transfers between devices, local(): lax.all_to_all(layer_out.reshape(owners, most, D), ('loader', 'pack'), sp...  30.5 us
    all_to_all x1, waiting for transfers between devices, local(): lax.all_to_all(outgoing.reshape(owners, most, D), ('loader', 'pack'), spl...  30 us
    all_gather x1, waiting for transfers between devices, local(): lax.all_gather(attn_in, 'pack', axis=1, tiled=True)  22.8 us
    dot_general x1, matrix products, local(): jnp.dot(inner, whole_down, preferred_element_type=jnp.float32)  20.9 us
    dot_general x16, matrix products, one_head(): jnp.einsum('ivn,inf->ivf', attention_weight, value_rows, preferred_elemen...  18.5 us
    squeeze x16, local copies, waits for them, and re-layouts, attend(): result = lax.map(one_head, heads)  15.9 us
  transfers between devices with their start and end apart: 7, of which 5 were waited for; matrix products, arithmetic and copies ran while one was open for 23% of the time, Pallas kernels for 0%

commit v1 on v0

v1 whole, which is shorter than its diff:
```python
import functools

import jax
import jax.numpy as jnp
from jax import lax
from jax.experimental import pallas as pl
from jax.experimental.pallas import tpu as pltpu
from jax.sharding import PartitionSpec as P

D = 1024
FIELDS = 11
PATCH = 256
ROWS = 384
OWNERS = 128
MOST = 6
SLOTS = 768
CHUNKS = D // 128
NB_OUT = 56
NB_BACK = 48
EPS = 1e-06
BIG = 1e30
EXP_SCALE = 1.4426950408889634 / 8.0
MESH = pl.DeviceIdType.MESH
F32 = jnp.float32
BF16 = jnp.bfloat16

PER_WEIGHT = 19


def device(x, y, c, z):
    return (((x % 4) * 4 + y % 4) * 2 + c % 2, z % 4)


def dot(a, b):
    return jnp.dot(a, b, preferred_element_type=F32)


def iota(shape, dim):
    return lax.broadcasted_iota(jnp.int32, shape, dim)


def kernel(
    patches_ref,
    embed_ref,
    route_ref,
    frame_ref,
    fields_ref,
    norm_attn_ref,
    norm_mlp_ref,
    attn_in_ref,
    attn_out_ref,
    mlp_in_ref,
    mlp_out_ref,
    out_ref,
    w_in,
    w_out,
    w_up,
    w_down,
    raw_in,
    embed_v,
    flat,
    embedded,
    stage,
    send_out,
    recv_out,
    send_back,
    recv_back,
    rows,
    normed,
    qkv,
    heads,
    hidden,
    total,
    gather,
    local_sem,
    row_sem,
    wsend,
    wrecv,
):
    loader = lax.axis_index("loader")
    z = lax.axis_index("pack")
    x, y, c = loader // 8, (loader // 2) % 4, loader % 2
    me = loader * 4 + z
    r = jnp.where(c == 0, x, y)

    loads = []

    def load(src, dst):
        copy = pltpu.make_async_copy(src, dst, local_sem.at[len(loads)])
        copy.start()
        loads.append(copy)
        return copy

    get_in = load(attn_in_ref, raw_in)
    get_embed = load(embed_ref, embed_v)
    get_patches = load(patches_ref, flat)
    get_out = load(attn_out_ref, w_out.at[z])
    get_up = load(mlp_in_ref, w_up.at[z])
    get_down = load(mlp_out_ref, w_down.at[z])

    def peer(k):
        dc, dx, dy, dz = k % 2, (k // 2) % 4, (k // 8) % 4, k // 32
        px, py, pc, pz = (x + dx) % 4, (y + dy) % 4, (c + dc) % 2, (z + dz) % 4
        to = (px * 4 + py) * 2 + pc
        return (to, pz), to * 4 + pz

    barrier = pltpu.get_barrier_semaphore()

    def greet(k, carry):
        pl.semaphore_signal(barrier, inc=1, device_id=peer(k)[0], device_id_type=MESH)
        return carry

    lax.fori_loop(1, OWNERS, greet, 0)

    get_in.wait()

    def reorder(n, carry):
        col = iota((768, 256), 1)
        source = (col >> 6) * 192 + n * 64 + (col & 63)
        pick = (iota((768, 256), 0) == source).astype(BF16)
        at = pl.multiple_of(n * 256, 256)
        w_in[z, :, pl.ds(at, 256)] = dot(raw_in[...], pick).astype(BF16)
        return carry

    lax.fori_loop(0, 3, reorder, 0)

    route_row = route_ref[...]
    frame_row = frame_ref[...].astype(F32)
    eye = iota((ROWS, ROWS), 0) == iota((ROWS, ROWS), 1)

    def column(row):
        return jnp.sum(jnp.where(eye, row, 0.0), axis=1, keepdims=True)

    onehot = (iota((OWNERS, ROWS), 0) == route_row).astype(F32)
    before = (iota((ROWS, ROWS), 0) < iota((ROWS, ROWS), 1)).astype(BF16)
    rank_row = jnp.sum(dot(onehot.astype(BF16), before) * onehot, axis=0, keepdims=True)
    route_col = column(route_row.astype(F32))
    rank_col = column(rank_row)
    fields_col = column(fields_ref[...].astype(F32))
    owner_lane = iota((ROWS, OWNERS), 1).astype(F32)
    for k in range(MOST):
        gather[:, k * OWNERS : (k + 1) * OWNERS] = (
            (owner_lane == route_col) & (rank_col == float(k))
        ).astype(BF16)

    get_embed.wait()
    get_patches.wait()
    for f in range(FIELDS):
        part = flat[f]
        flat[f] = jnp.where(fields_col > float(f), part.astype(F32), 0.0).astype(BF16)

    def embed_tile(n, carry):
        at = pl.multiple_of(n * 256, 256)
        acc = dot(flat[0], embed_v[0, :, pl.ds(at, 256)])
        for f in range(1, FIELDS):
            acc = acc + dot(flat[f], embed_v[f, :, pl.ds(at, 256)])
        embedded[:, pl.ds(at, 256)] = acc.astype(BF16)
        return carry

    lax.fori_loop(0, 4, embed_tile, 0)

    for k in range(MOST):
        place = onehot * (rank_row == float(k)).astype(F32)
        tag = jnp.sum(place * (frame_row + 1.0), axis=1, keepdims=True) - 1.0
        placed = dot(place.astype(BF16), embedded[...])
        for n in range(CHUNKS):
            stage[pl.ds(k * CHUNKS + n, OWNERS, stride=NB_OUT), :] = placed[
                :, n * 128 : (n + 1) * 128
            ]
        stage[pl.ds(48 + k, OWNERS, stride=NB_OUT), :] = jnp.broadcast_to(tag, (OWNERS, 128))
    for k in range(48 + MOST, NB_OUT):
        stage[pl.ds(k, OWNERS, stride=NB_OUT), :] = jnp.zeros((OWNERS, 128), F32)

    def pack_out(k, carry):
        at = pl.multiple_of(k * 8 * NB_OUT, 8 * NB_OUT)
        block = stage[pl.ds(at, 8 * NB_OUT), :]
        send_out[pl.ds(k * 8, 8)] = block.reshape(8, NB_OUT, 128).astype(BF16)
        return carry

    lax.fori_loop(0, OWNERS // 8, pack_out, 0)

    get_out.wait()
    get_up.wait()
    get_down.wait()
    pl.semaphore_wait(barrier, OWNERS - 1)

    weights = (w_in, w_out, w_up, w_down)
    copies = {}

    def send(w, slot, block, to):
        copy = pltpu.make_async_remote_copy(
            block,
            block,
            wsend.at[w * PER_WEIGHT + slot],
            wrecv.at[w * PER_WEIGHT + slot],
            device_id=to,
            device_id_type=MESH,
        )
        copy.start()
        copies[w, slot] = copy

    def arrived(w, slot):
        copies[w, slot].wait_recv()

    z_of = ((z + 3) % 4, (z + 1) % 4, (z + 2) % 4)
    up_z, down_z = device(x, y, c, z + 1), device(x, y, c, z + 3)
    one = jnp.where(c == 0, 1, 0)
    up_r = device(x + one, y + 1 - one, c, z)
    down_r = device(x + 3 * one, y + 3 - 3 * one, c, z)
    other = device(x, y, c + 1, z)

    def part(w, which, q, half=None):
        size = weights[w].shape[1] // 8
        start = (c * 4 + q % 4) * size
        if half is not None:
            size = size // 2
            start = start + half * size
        return weights[w].at[which, pl.ds(pl.multiple_of(start, size), size)]

    def begin(w):
        send(w, 0, part(w, z, r), up_z)
        send(w, 1, part(w, z, r), down_z)

    def ring(w, i):
        send(w, 4 + 4 * i, part(w, z_of[i], r), up_r)
        send(w, 5 + 4 * i, part(w, z_of[i], r), down_r)

    def near(w):
        arrived(w, 0)
        send(w, 2, part(w, z_of[0], r, 0), up_z)
        ring(w, 0)
        arrived(w, 1)
        send(w, 3, part(w, z_of[1], r, 1), down_z)
        ring(w, 1)

    def far(w):
        arrived(w, 2)
        arrived(w, 3)
        ring(w, 2)

    def onward(w, i):
        arrived(w, 4 + 4 * i)
        send(w, 6 + 4 * i, part(w, z_of[i], r + 3, 0), up_r)
        arrived(w, 5 + 4 * i)
        send(w, 7 + 4 * i, part(w, z_of[i], r + 1, 1), down_r)

    def share(w, i):
        arrived(w, 6 + 4 * i)
        arrived(w, 7 + 4 * i)
        size = weights[w].shape[1] // 2
        at = pl.multiple_of(c * size, size)
        send(w, 16 + i, weights[w].at[z_of[i], pl.ds(at, size)], other)

    def ready(w, i):
        arrived(w, 16 + i)

    def exchange(source, target, sems):
        own = pltpu.make_async_copy(source.at[me], target.at[me], sems[2])
        own.start()

        def one_peer(k, carry):
            to, index = peer(k)
            pltpu.make_async_remote_copy(
                source.at[index],
                target.at[me],
                sems[0],
                sems[1],
                device_id=to,
                device_id_type=MESH,
            ).start()
            return carry

        lax.fori_loop(1, OWNERS, one_peer, 0)
        return own

    def finish(source, target, sems, own):
        own.wait()
        pltpu.make_async_remote_copy(
            source.at[pl.ds(0, OWNERS - 1)],
            target.at[pl.ds(0, OWNERS - 1)],
            sems[0],
            sems[1],
            device_id=other,
            device_id_type=MESH,
        ).wait()

    sems_out = (row_sem.at[0], row_sem.at[1], row_sem.at[2])
    sems_back = (row_sem.at[3], row_sem.at[4], row_sem.at[5])

    begin(0)
    own_out = exchange(send_out, recv_out, sems_out)
    begin(1)
    begin(2)
    begin(3)
    near(0)
    far(0)
    near(1)
    onward(0, 0)
    onward(0, 1)
    onward(0, 2)
    near(2)
    share(0, 0)
    share(0, 1)
    share(0, 2)
    near(3)
    far(1)
    finish(send_out, recv_out, sems_out, own_out)

    def unpack_out(k, carry):
        at = pl.multiple_of(k * 8 * NB_OUT, 8 * NB_OUT)
        block = recv_out[pl.ds(k * 8, 8)].astype(F32)
        stage[pl.ds(at, 8 * NB_OUT), :] = block.reshape(8 * NB_OUT, 128)
        return carry

    lax.fori_loop(0, OWNERS // 8, unpack_out, 0)

    def norm_rows(k, carry):
        at = pl.multiple_of(k * OWNERS, OWNERS)
        square = jnp.zeros((OWNERS, 128), F32)
        for n in range(CHUNKS):
            part_rows = stage[pl.ds(k * CHUNKS + n, OWNERS, stride=NB_OUT), :]
            rows[pl.ds(at, OWNERS), n * 128 : (n + 1) * 128] = part_rows
            square = square + part_rows * part_rows
        mean = jnp.sum(square, axis=1, keepdims=True) * (1.0 / D)
        scaled = rows[pl.ds(at, OWNERS), :] * lax.rsqrt(mean + EPS) * norm_attn_ref[...]
        normed[pl.ds(at, OWNERS), :] = scaled.astype(BF16)
        return carry

    for k in range(MOST):
        norm_rows(k, 0)

    tags = jnp.concatenate(
        [stage[pl.ds(48 + k, OWNERS, stride=NB_OUT), :] for k in range(MOST)], axis=0
    )
    lane = iota((SLOTS, 128), 1)
    low = lane < 64
    same_tag = tags == ((lane & 63) - 1).astype(F32)
    tag_query = same_tag.astype(BF16)
    tag_key = jnp.where(same_tag | ((lane & 63) > 4), 0.0, -BIG).astype(BF16)

    def attend(which):
        def project(n, carry):
            at = pl.multiple_of(n * 256, 256)
            qkv[:, pl.ds(at, 256)] = dot(normed[...], w_in[which, :, pl.ds(at, 256)]).astype(BF16)
            return carry

        lax.fori_loop(0, 3, project, 0)

        def pair(p, carry):
            at = pl.multiple_of(p * 128, 128)
            query = qkv[:, pl.ds(at, 128)]
            key = qkv[:, pl.ds(at + 256, 128)]
            value = qkv[:, pl.ds(at + 512, 128)]
            results = []
            for h in range(2):
                mine = low if h == 0 else jnp.logical_not(low)
                keys = jnp.where(mine, key, tag_key)
                values = jnp.where(mine, value, jnp.ones_like(value))
                queries = jnp.where(mine, query, tag_query)
                blocks = []
                for b in range(3):
                    scores = lax.dot_general(
                        queries[b * 256 : (b + 1) * 256],
                        keys,
                        (((1,), (1,)), ((), ())),
                        preferred_element_type=F32,
                    )
                    highest = jnp.max(scores, axis=1, keepdims=True)
                    shifted = jnp.exp2((scores - highest) * EXP_SCALE).astype(BF16)
                    blocks.append(dot(shifted, values))
                results.append(blocks)
            for b in range(3):
                half = low[:256]
                top = jnp.where(half, results[0][b], results[1][b])
                sums = jnp.where(half, results[1][b], results[0][b])
                heads[which * 2 + p, b * 256 : (b + 1) * 256, :] = top / pltpu.roll(sums, 64, 1)
            return carry

        lax.fori_loop(0, 2, pair, 0)

    attend(z)
    far(2)
    onward(1, 0)
    onward(1, 1)
    onward(1, 2)
    ready(0, 0)
    attend(z_of[0])
    far(3)
    onward(2, 0)
    onward(2, 1)
    share(1, 0)
    share(1, 1)
    share(1, 2)
    ready(0, 1)
    attend(z_of[1])
    onward(2, 2)
    onward(3, 0)
    share(2, 0)
    share(2, 1)
    ready(0, 2)
    attend(z_of[2])

    for k in range(MOST):
        for n in range(CHUNKS):
            stage[pl.ds(k * CHUNKS + n, OWNERS, stride=NB_BACK), :] = heads[
                n, k * OWNERS : (k + 1) * OWNERS, :
            ]

    def pack_back(k, carry):
        at = pl.multiple_of(k * 8 * NB_BACK, 8 * NB_BACK)
        block = stage[pl.ds(at, 8 * NB_BACK), :]
        send_back[pl.ds(k * 8, 8)] = block.reshape(8, NB_BACK, 128).astype(BF16)
        return carry

    lax.fori_loop(0, OWNERS // 8, pack_back, 0)
    own_back = exchange(send_back, recv_back, sems_back)
    onward(3, 1)
    onward(3, 2)
    share(2, 2)
    share(3, 0)
    share(3, 1)
    share(3, 2)
    for i in range(3):
        ready(1, i)
    finish(send_back, recv_back, sems_back, own_back)

    def unpack_back(k, carry):
        at = pl.multiple_of(k * 8 * NB_BACK, 8 * NB_BACK)
        block = recv_back[pl.ds(k * 8, 8)].astype(F32)
        stage[pl.ds(at, 8 * NB_BACK), :] = block.reshape(8 * NB_BACK, 128)
        return carry

    lax.fori_loop(0, OWNERS // 8, unpack_back, 0)
    for k in range(MOST):
        for n in range(CHUNKS):
            normed[k * OWNERS : (k + 1) * OWNERS, n * 128 : (n + 1) * 128] = stage[
                pl.ds(k * CHUNKS + n, OWNERS, stride=NB_BACK), :
            ].astype(BF16)

    def take(n, carry):
        at = pl.multiple_of(n * 256, 256)
        qkv[0:ROWS, pl.ds(0, 256)] = dot(gather[...], normed[:, pl.ds(at, 256)]).astype(BF16)
        partial = qkv[0:ROWS, pl.ds(0, 256)]
        for m in range(4):
            to = slice(m * 256, (m + 1) * 256)
            hidden[:, to] = hidden[:, to] + dot(partial, w_out[n, :, to])
        return carry

    hidden[...] = embedded[...].astype(F32)
    lax.fori_loop(0, 4, take, 0)
    values = hidden[...]
    mean = jnp.sum(values * values, axis=1, keepdims=True) * (1.0 / D)
    normed[0:ROWS, :] = (values * lax.rsqrt(mean + EPS) * norm_mlp_ref[...]).astype(BF16)
    total[...] = hidden[...]

    def mlp(which):
        def widen(n, carry):
            at = pl.multiple_of(n * 256, 256)
            up = dot(normed[0:ROWS, :], w_up[which, :, pl.ds(at, 256)])
            normed[ROWS:SLOTS, pl.ds(at, 256)] = jax.nn.gelu(up).astype(BF16)
            return carry

        lax.fori_loop(0, 4, widen, 0)

        def narrow(n, carry):
            at = pl.multiple_of(n * 256, 256)
            total[:, pl.ds(at, 256)] = total[:, pl.ds(at, 256)] + dot(
                normed[ROWS:SLOTS, :], w_down[which, :, pl.ds(at, 256)]
            )
            return carry

        lax.fori_loop(0, 4, narrow, 0)

    mlp(z)
    for i in range(3):
        ready(2, i)
        ready(3, i)
        mlp(z_of[i])
    out_ref[...] = total[...].astype(BF16)
    for copy in copies.values():
        copy.wait_send()


def local(
    patches, fields, route, frame, embed, norm_attn, attn_in, attn_out, norm_mlp, mlp_in, mlp_out
):
    by_field = jnp.transpose(patches, (1, 0, 2))
    whole = pl.BlockSpec(memory_space=pl.ANY)
    vmem = pl.BlockSpec(memory_space=pltpu.VMEM)
    return pl.pallas_call(
        kernel,
        out_shape=jax.ShapeDtypeStruct((ROWS, D), BF16),
        in_specs=[whole, whole, vmem, vmem, vmem, vmem, vmem, whole, whole, whole, whole],
        out_specs=vmem,
        scratch_shapes=[
            pltpu.VMEM((4, D, 768), BF16),
            pltpu.VMEM((4, 256, D), BF16),
            pltpu.VMEM((4, D, D), BF16),
            pltpu.VMEM((4, D, D), BF16),
            pltpu.VMEM((D, 768), BF16),
            pltpu.VMEM((FIELDS, PATCH, D), BF16),
            pltpu.VMEM((FIELDS, ROWS, PATCH), BF16),
            pltpu.VMEM((ROWS, D), BF16),
            pltpu.VMEM((OWNERS * NB_OUT, 128), F32),
            pltpu.VMEM((OWNERS, NB_OUT, 128), BF16),
            pltpu.VMEM((OWNERS, NB_OUT, 128), BF16),
            pltpu.VMEM((OWNERS, NB_BACK, 128), BF16),
            pltpu.VMEM((OWNERS, NB_BACK, 128), BF16),
            pltpu.VMEM((SLOTS, D), F32),
            pltpu.VMEM((SLOTS, D), BF16),
            pltpu.VMEM((SLOTS, 768), BF16),
            pltpu.VMEM((CHUNKS, SLOTS, 128), F32),
            pltpu.VMEM((ROWS, D), F32),
            pltpu.VMEM((ROWS, D), F32),
            pltpu.VMEM((ROWS, SLOTS), BF16),
            pltpu.SemaphoreType.DMA((6,)),
            pltpu.SemaphoreType.DMA((6,)),
            pltpu.SemaphoreType.DMA((4 * PER_WEIGHT,)),
            pltpu.SemaphoreType.DMA((4 * PER_WEIGHT,)),
        ],
        compiler_params=pltpu.CompilerParams(
            collective_id=0, has_side_effects=True, vmem_limit_bytes=62 * 1024 * 1024
        ),
        cost_estimate=pl.CostEstimate(
            flops=25_000_000_000, bytes_accessed=16_000_000, transcendentals=11_000_000
        ),
    )(
        by_field,
        embed,
        route.reshape(1, ROWS),
        frame.reshape(1, ROWS),
        fields.reshape(1, ROWS),
        norm_attn.reshape(1, D),
        norm_mlp.reshape(1, D),
        attn_in,
        attn_out,
        mlp_in,
        mlp_out,
    )


def solution(mesh):
    return jax.shard_map(
        local,
        mesh=mesh,
        in_specs=(
            P(("loader", "pack"), None, None),
            P(("loader", "pack")),
            P(("loader", "pack")),
            P(("loader", "pack")),
            P(),
            P(),
            P(None, "pack"),
            P("pack", None),
            P(),
            P(None, "pack"),
            P("pack", None),
        ),
        out_specs=P(("loader", "pack"), None),
        check_vma=False,
    )
```

time: 381 us -> 153 us (0.40)
  waiting for transfers between devices: 218 us -> 0 us
  Pallas kernels: 0 us -> 147 us
  matrix products: 69.5 us -> 0 us
  local copies, waits for them, and re-layouts: 39.8 us -> 5.83 us
  starting transfers between devices: 31 us -> 0 us
  between operations: 13.3 us -> 0.01 us
  other arithmetic: 7.3 us -> 0 us
    all_gather x4 -> x0, waiting for transfers between devices: 156 us -> none  [the longest x1 85.7 us: local(): lax.all_gather(mlp_in, 'pack', axis=1, tiled=True)]
    pallas_call x0 -> x1, Pallas kernels: none -> 147 us  [local(): pl.pallas_call(kernel, out_shape=jax.ShapeDtypeStruct((ROWS, D), BF16), i...]
    dot_general x36 -> x0, matrix products: 69.5 us -> none  [the longest x1 20.9 us: local(): jnp.dot(inner, whole_down, preferred_element_type=jnp.float32)]
    all_to_all x3 -> x0, waiting for transfers between devices: 60.4 us -> none  [the longest x1 30.5 us: local(): lax.all_to_all(layer_out.reshape(owners, most, D), ('loader', 'pack'), sp...]
    all_to_all x3 -> x0, starting transfers between devices: 30.7 us -> none  [the longest x1 11.5 us: local(): lax.all_to_all(labels.reshape(owners, most), ('loader', 'pack'), split_ax...]
    squeeze x16 -> x0, local copies, waits for them, and re-layouts: 15.9 us -> none  [attend(): result = lax.map(one_head, heads)]
    convert_element_type x3 -> x0, local copies, waits for them, and re-layouts: 8.75 us -> none  [the longest x1 6.64 us: local(): jnp.dot(normed, whole_in, preferred_element_type=jnp.float32)]
    reduce_sum x18 -> x0, other arithmetic: 6.75 us -> none  [the longest x16 5.91 us: one_head(): jnp.sum(shifted, axis=-1, keepdims=True)]
  transfers between devices with their start and end apart: 7 -> 0, of which waited for: 5 -> 0; matrix products, arithmetic and copies ran while one was open for 23% -> 0% of each run, Pallas kernels for 0% -> 0%
where the time goes in v1:
time: 153 us
  Pallas kernels  147 us (96%)
  local copies, waits for them, and re-layouts  5.83 us (4%)
    pallas_call x1, Pallas kernels, local(): pl.pallas_call(kernel, out_shape=jax.ShapeDtypeStruct((ROWS, D), BF16), i...  147 us

profile of v1, /device:TPU:1, one launch (start us, length us, event | category | flops | bytes accessed | tf_op | source)
XLA Modules:
  0.0 153.1 jit_solution(9113862791254770041)
XLA Ops:
  0.0 1.3 reshape.17.fields_ref
  1.3 1.2 reshape.15.route_ref
  2.5 1.3 reshape.16.frame_ref
  3.8 147.3 %shard_map.109 = bf16[384,1024]{1,0:T(8,128)(2,1)} custom-call(bf16[11,384,256]{2,1,0:T(8,128)(2,1)} %bitcast.3, bf16[11,256,1024]{2,1,0:T(8,128)(2,1)} %embed_ref.1, s32[1,384]{1,0:T(1,128)} %reshape.15.route_ref, s32[1,384]{1,0:T(1,128)} %reshape.16.frame_ref, s32[1,384]{1,0:T(1,128)} %reshape.17.fields_ref, f32[1,1024]{1,0:T(1,128)} %bitcast.4, ...), custom_call_target="tpu_custom_call" | custom-call | flops 24999999488 | bytes 16000000 | tf_op jit(solution)/shard_map/pallas_call | solution.py:490
  151.0 2.1 %copy.13 = bf16[384,1024]{1,0:T(8,128)(2,1)} copy(bf16[384,1024]{1,0:T(8,128)(2,1)} %shard_map.109) | data formatting | bytes 1572864

commit v2 on v1

--- a/solution.py
+++ b/solution.py
@@ -76,6 +76,7 @@
     row_sem,
     wsend,
     wrecv,
+    here,
 ):
     loader = lax.axis_index("loader")
     z = lax.axis_index("pack")
@@ -99,18 +100,25 @@
     get_down = load(mlp_out_ref, w_down.at[z])
 
     def peer(k):
-        dc, dx, dy, dz = k % 2, (k // 2) % 4, (k // 8) % 4, k // 32
+        dx, dc = k % 4, (k // 64 + k) % 2
+        dy, dz = (k // 4 + dx) % 4, (k // 16 + 4 - dx) % 4
         px, py, pc, pz = (x + dx) % 4, (y + dy) % 4, (c + dc) % 2, (z + dz) % 4
         to = (px * 4 + py) * 2 + pc
         return (to, pz), to * 4 + pz
 
     barrier = pltpu.get_barrier_semaphore()
-
-    def greet(k, carry):
-        pl.semaphore_signal(barrier, inc=1, device_id=peer(k)[0], device_id_type=MESH)
-        return carry
-
-    lax.fori_loop(1, OWNERS, greet, 0)
+    line_x = [device(x + k, y, c, z) for k in (1, 3, 2)]
+    line_y = [device(x, y + k, c, z) for k in (1, 3, 2)]
+    line_z = [device(x, y, c, z + k) for k in (1, 3, 2)]
+    for to in line_x + line_y + line_z + [device(x, y, c + 1, z)]:
+        pl.semaphore_signal(barrier, inc=1, device_id=to, device_id_type=MESH)
+
+    def greet(line, stage):
+        for to in line:
+            pl.semaphore_signal(here.at[stage], inc=1, device_id=to, device_id_type=MESH)
+
+    def heard(stage):
+        pl.semaphore_wait(here.at[stage], 3)
 
     get_in.wait()
 
@@ -124,8 +132,96 @@
 
     lax.fori_loop(0, 3, reorder, 0)
 
-    route_row = route_ref[...]
-    frame_row = frame_ref[...].astype(F32)
+    weights = (w_in, w_out, w_up, w_down)
+    z_of = ((z + 3) % 4, (z + 1) % 4, (z + 2) % 4)
+    up_z, down_z = device(x, y, c, z + 1), device(x, y, c, z + 3)
+    one = jnp.where(c == 0, 1, 0)
+    up_r = device(x + one, y + 1 - one, c, z)
+    down_r = device(x + 3 * one, y + 3 - 3 * one, c, z)
+    other = device(x, y, c + 1, z)
+
+    def part(w, which, q, half=None):
+        size = weights[w].shape[1] // 8
+        start = (c * 4 + q % 4) * size
+        if half is not None:
+            size = size // 2
+            start = start + half * size
+        return weights[w].at[which, pl.ds(pl.multiple_of(start, size), size)]
+
+    def copy_of(w, slot):
+        if slot < 2:
+            block, to = part(w, z, r), (up_z, down_z)[slot]
+        elif slot < 4:
+            block, to = part(w, z_of[slot - 2], r, slot - 2), (up_z, down_z)[slot - 2]
+        elif slot < 16:
+            i, step = (slot - 4) // 4, (slot - 4) % 4
+            to = (up_r, down_r)[step % 2]
+            if step < 2:
+                block = part(w, z_of[i], r)
+            else:
+                block = part(w, z_of[i], r + (3 if step == 2 else 1), step - 2)
+        else:
+            size = weights[w].shape[1] // 2
+            at = pl.multiple_of(c * size, size)
+            block, to = weights[w].at[z_of[slot - 16], pl.ds(at, size)], other
+        return pltpu.make_async_remote_copy(
+            block,
+            block,
+            wsend.at[w * PER_WEIGHT + slot],
+            wrecv.at[w * PER_WEIGHT + slot],
+            device_id=to,
+            device_id_type=MESH,
+        )
+
+    def send(w, slot):
+        copy_of(w, slot).start()
+
+    def arrived(w, slot):
+        copy_of(w, slot).wait_recv()
+
+    def begin(w):
+        send(w, 0)
+        send(w, 1)
+
+    def ring(w, i):
+        send(w, 4 + 4 * i)
+        send(w, 5 + 4 * i)
+
+    def near(w):
+        arrived(w, 0)
+        send(w, 2)
+        ring(w, 0)
+        arrived(w, 1)
+        send(w, 3)
+        ring(w, 1)
+
+    def far(w):
+        arrived(w, 2)
+        arrived(w, 3)
+        ring(w, 2)
+
+    def onward(w, i):
+        arrived(w, 4 + 4 * i)
+        send(w, 6 + 4 * i)
+        arrived(w, 5 + 4 * i)
+        send(w, 7 + 4 * i)
+
+    def share(w, i):
+        arrived(w, 6 + 4 * i)
+        arrived(w, 7 + 4 * i)
+        send(w, 16 + i)
+
+    def ready(w, i):
+        arrived(w, 16 + i)
+
+    pl.semaphore_wait(barrier, 10)
+    begin(0)
+    greet(line_z, 0)
+    get_out.wait()
+    begin(1)
+
+    route_row = route_ref[...].reshape(1, ROWS)
+    frame_row = frame_ref[...].reshape(1, ROWS).astype(F32)
     eye = iota((ROWS, ROWS), 0) == iota((ROWS, ROWS), 1)
 
     def column(row):
@@ -136,18 +232,21 @@
     rank_row = jnp.sum(dot(onehot.astype(BF16), before) * onehot, axis=0, keepdims=True)
     route_col = column(route_row.astype(F32))
     rank_col = column(rank_row)
-    fields_col = column(fields_ref[...].astype(F32))
+    fields_col = column(fields_ref[...].reshape(1, ROWS).astype(F32))
     owner_lane = iota((ROWS, OWNERS), 1).astype(F32)
     for k in range(MOST):
         gather[:, k * OWNERS : (k + 1) * OWNERS] = (
             (owner_lane == route_col) & (rank_col == float(k))
         ).astype(BF16)
 
+    heard(0)
+    greet(line_y, 1)
+
     get_embed.wait()
     get_patches.wait()
     for f in range(FIELDS):
-        part = flat[f]
-        flat[f] = jnp.where(fields_col > float(f), part.astype(F32), 0.0).astype(BF16)
+        pixels = flat[f]
+        flat[f] = jnp.where(fields_col > float(f), pixels.astype(F32), 0.0).astype(BF16)
 
     def embed_tile(n, carry):
         at = pl.multiple_of(n * 256, 256)
@@ -158,6 +257,10 @@
         return carry
 
     lax.fori_loop(0, 4, embed_tile, 0)
+
+    heard(1)
+    greet(line_x, 2)
+    near(0)
 
     for k in range(MOST):
         place = onehot * (rank_row == float(k)).astype(F32)
@@ -179,80 +282,12 @@
 
     lax.fori_loop(0, OWNERS // 8, pack_out, 0)
 
-    get_out.wait()
+    heard(2)
+    near(1)
     get_up.wait()
-    get_down.wait()
-    pl.semaphore_wait(barrier, OWNERS - 1)
-
-    weights = (w_in, w_out, w_up, w_down)
-    copies = {}
-
-    def send(w, slot, block, to):
-        copy = pltpu.make_async_remote_copy(
-            block,
-            block,
-            wsend.at[w * PER_WEIGHT + slot],
-            wrecv.at[w * PER_WEIGHT + slot],
-            device_id=to,
-            device_id_type=MESH,
-        )
-        copy.start()
-        copies[w, slot] = copy
-
-    def arrived(w, slot):
-        copies[w, slot].wait_recv()
-
-    z_of = ((z + 3) % 4, (z + 1) % 4, (z + 2) % 4)
-    up_z, down_z = device(x, y, c, z + 1), device(x, y, c, z + 3)
-    one = jnp.where(c == 0, 1, 0)
-    up_r = device(x + one, y + 1 - one, c, z)
-    down_r = device(x + 3 * one, y + 3 - 3 * one, c, z)
-    other = device(x, y, c + 1, z)
-
-    def part(w, which, q, half=None):
-        size = weights[w].shape[1] // 8
-        start = (c * 4 + q % 4) * size
-        if half is not None:
-            size = size // 2
-            start = start + half * size
-        return weights[w].at[which, pl.ds(pl.multiple_of(start, size), size)]
-
-    def begin(w):
-        send(w, 0, part(w, z, r), up_z)
-        send(w, 1, part(w, z, r), down_z)
-
-    def ring(w, i):
-        send(w, 4 + 4 * i, part(w, z_of[i], r), up_r)
-        send(w, 5 + 4 * i, part(w, z_of[i], r), down_r)
-
-    def near(w):
-        arrived(w, 0)
-        send(w, 2, part(w, z_of[0], r, 0), up_z)
-        ring(w, 0)
-        arrived(w, 1)
-        send(w, 3, part(w, z_of[1], r, 1), down_z)
-        ring(w, 1)
-
-    def far(w):
-        arrived(w, 2)
-        arrived(w, 3)
-        ring(w, 2)
-
-    def onward(w, i):
-        arrived(w, 4 + 4 * i)
-        send(w, 6 + 4 * i, part(w, z_of[i], r + 3, 0), up_r)
-        arrived(w, 5 + 4 * i)
-        send(w, 7 + 4 * i, part(w, z_of[i], r + 1, 1), down_r)
-
-    def share(w, i):
-        arrived(w, 6 + 4 * i)
-        arrived(w, 7 + 4 * i)
-        size = weights[w].shape[1] // 2
-        at = pl.multiple_of(c * size, size)
-        send(w, 16 + i, weights[w].at[z_of[i], pl.ds(at, size)], other)
-
-    def ready(w, i):
-        arrived(w, 16 + i)
+    begin(2)
+    far(0)
+    far(1)
 
     def exchange(source, target, sems):
         own = pltpu.make_async_copy(source.at[me], target.at[me], sems[2])
@@ -287,23 +322,19 @@
     sems_out = (row_sem.at[0], row_sem.at[1], row_sem.at[2])
     sems_back = (row_sem.at[3], row_sem.at[4], row_sem.at[5])
 
-    begin(0)
     own_out = exchange(send_out, recv_out, sems_out)
-    begin(1)
-    begin(2)
+    for i in range(3):
+        onward(0, i)
+    near(2)
+    for i in range(3):
+        share(0, i)
+    get_down.wait()
     begin(3)
-    near(0)
-    far(0)
-    near(1)
-    onward(0, 0)
-    onward(0, 1)
-    onward(0, 2)
-    near(2)
-    share(0, 0)
-    share(0, 1)
-    share(0, 2)
-    near(3)
-    far(1)
+    for i in range(3):
+        onward(1, i)
+    far(2)
+    for i in range(3):
+        share(1, i)
     finish(send_out, recv_out, sems_out, own_out)
 
     def unpack_out(k, carry):
@@ -338,7 +369,21 @@
     tag_query = same_tag.astype(BF16)
     tag_key = jnp.where(same_tag | ((lane & 63) > 4), 0.0, -BIG).astype(BF16)
 
-    def attend(which):
+    def shard(step):
+        which = jnp.where(step == 1, z_of[0], jnp.where(step == 2, z_of[1], z_of[2]))
+        return jnp.where(step == 0, z, which)
+
+    def at_step(step, now, *actions):
+        @pl.when(step == now)
+        def _():
+            for action, *given in actions:
+                action(*given)
+
+    def attend(step, carry):
+        which = shard(step)
+        for i in range(3):
+            at_step(step, i + 1, (ready, 0, i))
+
         def project(n, carry):
             at = pl.multiple_of(n * 256, 256)
             qkv[:, pl.ds(at, 256)] = dot(normed[...], w_in[which, :, pl.ds(at, 256)]).astype(BF16)
@@ -374,31 +419,24 @@
                 top = jnp.where(half, results[0][b], results[1][b])
                 sums = jnp.where(half, results[1][b], results[0][b])
                 heads[which * 2 + p, b * 256 : (b + 1) * 256, :] = top / pltpu.roll(sums, 64, 1)
+            for now in range(8):
+                at_step(step * 2 + p, now, *schedule[now])
             return carry
 
         lax.fori_loop(0, 2, pair, 0)
-
-    attend(z)
-    far(2)
-    onward(1, 0)
-    onward(1, 1)
-    onward(1, 2)
-    ready(0, 0)
-    attend(z_of[0])
-    far(3)
-    onward(2, 0)
-    onward(2, 1)
-    share(1, 0)
-    share(1, 1)
-    share(1, 2)
-    ready(0, 1)
-    attend(z_of[1])
-    onward(2, 2)
-    onward(3, 0)
-    share(2, 0)
-    share(2, 1)
-    ready(0, 2)
-    attend(z_of[2])
+        return carry
+
+    schedule = (
+        [(near, 3), (onward, 2, 0)],
+        [(onward, 2, 1), (onward, 2, 2)],
+        [(far, 3), (share, 2, 0), (share, 2, 1)],
+        [(share, 2, 2), (onward, 3, 0)],
+        [(onward, 3, 1)],
+        [(onward, 3, 2), (share, 3, 0)],
+        [(share, 3, 1)],
+        [(share, 3, 2)],
+    )
+    lax.fori_loop(0, 4, attend, 0)
 
     for k in range(MOST):
         for n in range(CHUNKS):
@@ -414,12 +452,6 @@
 
     lax.fori_loop(0, OWNERS // 8, pack_back, 0)
     own_back = exchange(send_back, recv_back, sems_back)
-    onward(3, 1)
-    onward(3, 2)
-    share(2, 2)
-    share(3, 0)
-    share(3, 1)
-    share(3, 2)
     for i in range(3):
         ready(1, i)
     finish(send_back, recv_back, sems_back, own_back)
@@ -453,7 +485,11 @@
     normed[0:ROWS, :] = (values * lax.rsqrt(mean + EPS) * norm_mlp_ref[...]).astype(BF16)
     total[...] = hidden[...]
 
-    def mlp(which):
+    def mlp(step, carry):
+        which = shard(step)
+        for i in range(3):
+            at_step(step, i + 1, (ready, 2, i), (ready, 3, i))
+
         def widen(n, carry):
             at = pl.multiple_of(n * 256, 256)
             up = dot(normed[0:ROWS, :], w_up[which, :, pl.ds(at, 256)])
@@ -470,15 +506,13 @@
             return carry
 
         lax.fori_loop(0, 4, narrow, 0)
-
-    mlp(z)
-    for i in range(3):
-        ready(2, i)
-        ready(3, i)
-        mlp(z_of[i])
+        return carry
+
+    lax.fori_loop(0, 4, mlp, 0)
     out_ref[...] = total[...].astype(BF16)
-    for copy in copies.values():
-        copy.wait_send()
+    for w in range(4):
+        for slot in range(PER_WEIGHT):
+            copy_of(w, slot).wait_send()
 
 
 def local(
@@ -517,6 +551,7 @@
             pltpu.SemaphoreType.DMA((6,)),
             pltpu.SemaphoreType.DMA((4 * PER_WEIGHT,)),
             pltpu.SemaphoreType.DMA((4 * PER_WEIGHT,)),
+            pltpu.SemaphoreType.REGULAR((3,)),
         ],
         compiler_params=pltpu.CompilerParams(
             collective_id=0, has_side_effects=True, vmem_limit_bytes=62 * 1024 * 1024
@@ -527,9 +562,9 @@
     )(
         by_field,
         embed,
-        route.reshape(1, ROWS),
-        frame.reshape(1, ROWS),
-        fields.reshape(1, ROWS),
+        route,
+        frame,
+        fields,
         norm_attn.reshape(1, D),
         norm_mlp.reshape(1, D),
         attn_in,

time: 153 us -> 136 us (0.89)
  Pallas kernels: 147 us -> 133 us
  local copies, waits for them, and re-layouts: 5.83 us -> 2.06 us
    pallas_call x1, Pallas kernels: 147 us -> 133 us  [local(): pl.pallas_call(kernel, out_shape=jax.ShapeDtypeStruct((ROWS, D), BF16), i...]
    reshape x3 -> x0, local copies, waits for them, and re-layouts: 3.77 us -> none  [the longest x1 1.27 us: local(): fields.reshape(1, ROWS)]
where the time goes in v2:
time: 136 us; the launch traced here: 135 us
  Pallas kernels  133 us (98%)
  local copies, waits for them, and re-layouts  2.06 us (2%)
    pallas_call x1, Pallas kernels, local(): pl.pallas_call(kernel, out_shape=jax.ShapeDtypeStruct((ROWS, D), BF16), i...  133 us

profile of v2, /device:TPU:1, one launch (start us, length us, event | category | flops | bytes accessed | tf_op | source)
XLA Modules:
  0.0 135.4 jit_solution(31532691553404367)
XLA Ops:
  0.0 133.3 %shard_map.109 = bf16[384,1024]{1,0:T(8,128)(2,1)} custom-call(bf16[11,384,256]{2,1,0:T(8,128)(2,1)} %bitcast.3, bf16[11,256,1024]{2,1,0:T(8,128)(2,1)} %embed_ref.1, s32[384]{0:T(512)} %route_ref.1, s32[384]{0:T(512)} %frame_ref.1, s32[384]{0:T(512)} %fields_ref.1, f32[1,1024]{1,0:T(1,128)} %bitcast.4, f32[1,1024]{1,0:T(1,128)} %bitcast.5, ...), custom_call_target="tpu_custom_call" | custom-call | flops 24999999488 | bytes 16000000 | tf_op jit(solution)/shard_map/pallas_call | solution.py:524
  133.4 2.1 %copy.13 = bf16[384,1024]{1,0:T(8,128)(2,1)} copy(bf16[384,1024]{1,0:T(8,128)(2,1)} %shard_map.109) | data formatting | bytes 1572864

commit v3 on v2

--- a/solution.py
+++ b/solution.py
@@ -24,7 +24,8 @@
 F32 = jnp.float32
 BF16 = jnp.bfloat16
 
-PER_WEIGHT = 19
+PER_WEIGHT = 23
+WIDE = (3,)
 
 
 def device(x, y, c, z):
@@ -160,10 +161,14 @@
                 block = part(w, z_of[i], r)
             else:
                 block = part(w, z_of[i], r + (3 if step == 2 else 1), step - 2)
-        else:
+        elif slot < 19:
             size = weights[w].shape[1] // 2
             at = pl.multiple_of(c * size, size)
             block, to = weights[w].at[z_of[slot - 16], pl.ds(at, size)], other
+        elif slot < 21:
+            block, to = part(w, z, r + 2), (up_z, down_z)[slot - 19]
+        else:
+            block, to = part(w, z_of[slot - 21], r + 2, slot - 21), (up_z, down_z)[slot - 21]
         return pltpu.make_async_remote_copy(
             block,
             block,
@@ -179,9 +184,17 @@
     def arrived(w, slot):
         copy_of(w, slot).wait_recv()
 
+    def slots_of(w):
+        if w in WIDE:
+            return [k for k in range(PER_WEIGHT) if k < 4 or k >= 16 or k % 4 < 2]
+        return range(19)
+
     def begin(w):
         send(w, 0)
         send(w, 1)
+        if w in WIDE:
+            send(w, 19)
+            send(w, 20)
 
     def ring(w, i):
         send(w, 4 + 4 * i)
@@ -194,21 +207,32 @@
         arrived(w, 1)
         send(w, 3)
         ring(w, 1)
+        if w in WIDE:
+            arrived(w, 19)
+            send(w, 21)
+            arrived(w, 20)
+            send(w, 22)
 
     def far(w):
         arrived(w, 2)
         arrived(w, 3)
         ring(w, 2)
+        if w in WIDE:
+            arrived(w, 21)
+            arrived(w, 22)
 
     def onward(w, i):
+        if w in WIDE:
+            return
         arrived(w, 4 + 4 * i)
         send(w, 6 + 4 * i)
         arrived(w, 5 + 4 * i)
         send(w, 7 + 4 * i)
 
     def share(w, i):
-        arrived(w, 6 + 4 * i)
-        arrived(w, 7 + 4 * i)
+        last = 4 if w in WIDE else 6
+        arrived(w, last + 4 * i)
+        arrived(w, last + 1 + 4 * i)
         send(w, 16 + i)
 
     def ready(w, i):
@@ -218,7 +242,6 @@
     begin(0)
     greet(line_z, 0)
     get_out.wait()
-    begin(1)
 
     route_row = route_ref[...].reshape(1, ROWS)
     frame_row = frame_ref[...].reshape(1, ROWS).astype(F32)
@@ -230,16 +253,8 @@
     onehot = (iota((OWNERS, ROWS), 0) == route_row).astype(F32)
     before = (iota((ROWS, ROWS), 0) < iota((ROWS, ROWS), 1)).astype(BF16)
     rank_row = jnp.sum(dot(onehot.astype(BF16), before) * onehot, axis=0, keepdims=True)
-    route_col = column(route_row.astype(F32))
-    rank_col = column(rank_row)
+    heard(0)
     fields_col = column(fields_ref[...].reshape(1, ROWS).astype(F32))
-    owner_lane = iota((ROWS, OWNERS), 1).astype(F32)
-    for k in range(MOST):
-        gather[:, k * OWNERS : (k + 1) * OWNERS] = (
-            (owner_lane == route_col) & (rank_col == float(k))
-        ).astype(BF16)
-
-    heard(0)
     greet(line_y, 1)
 
     get_embed.wait()
@@ -249,14 +264,14 @@
         flat[f] = jnp.where(fields_col > float(f), pixels.astype(F32), 0.0).astype(BF16)
 
     def embed_tile(n, carry):
-        at = pl.multiple_of(n * 256, 256)
-        acc = dot(flat[0], embed_v[0, :, pl.ds(at, 256)])
+        at = pl.multiple_of(n * 1024, 1024)
+        acc = dot(flat[0], embed_v[0, :, pl.ds(at, 1024)])
         for f in range(1, FIELDS):
-            acc = acc + dot(flat[f], embed_v[f, :, pl.ds(at, 256)])
-        embedded[:, pl.ds(at, 256)] = acc.astype(BF16)
-        return carry
-
-    lax.fori_loop(0, 4, embed_tile, 0)
+            acc = acc + dot(flat[f], embed_v[f, :, pl.ds(at, 1024)])
+        embedded[:, pl.ds(at, 1024)] = acc.astype(BF16)
+        return carry
+
+    lax.fori_loop(0, 1, embed_tile, 0)
 
     heard(1)
     greet(line_x, 2)
@@ -283,11 +298,6 @@
     lax.fori_loop(0, OWNERS // 8, pack_out, 0)
 
     heard(2)
-    near(1)
-    get_up.wait()
-    begin(2)
-    far(0)
-    far(1)
 
     def exchange(source, target, sems):
         own = pltpu.make_async_copy(source.at[me], target.at[me], sems[2])
@@ -323,18 +333,24 @@
     sems_back = (row_sem.at[3], row_sem.at[4], row_sem.at[5])
 
     own_out = exchange(send_out, recv_out, sems_out)
-    for i in range(3):
-        onward(0, i)
-    near(2)
-    for i in range(3):
-        share(0, i)
+    route_col = column(route_row.astype(F32))
+    rank_col = column(rank_row)
+    owner_lane = iota((ROWS, OWNERS), 1).astype(F32)
+    for k in range(MOST):
+        gather[:, k * OWNERS : (k + 1) * OWNERS] = (
+            (owner_lane == route_col) & (rank_col == float(k))
+        ).astype(BF16)
+    begin(1)
+    get_up.wait()
     get_down.wait()
-    begin(3)
-    for i in range(3):
-        onward(1, i)
-    far(2)
-    for i in range(3):
-        share(1, i)
+    begin(2)
+    far(0)
+    onward(0, 0)
+    onward(0, 1)
+    onward(0, 2)
+    share(0, 0)
+    share(0, 1)
+    share(0, 2)
     finish(send_out, recv_out, sems_out, own_out)
 
     def unpack_out(k, carry):
@@ -385,11 +401,11 @@
             at_step(step, i + 1, (ready, 0, i))
 
         def project(n, carry):
-            at = pl.multiple_of(n * 256, 256)
-            qkv[:, pl.ds(at, 256)] = dot(normed[...], w_in[which, :, pl.ds(at, 256)]).astype(BF16)
+            at = pl.multiple_of(n * 768, 768)
+            qkv[:, pl.ds(at, 768)] = dot(normed[...], w_in[which, :, pl.ds(at, 768)]).astype(BF16)
             return carry
 
-        lax.fori_loop(0, 3, project, 0)
+        lax.fori_loop(0, 1, project, 0)
 
         def pair(p, carry):
             at = pl.multiple_of(p * 128, 128)
@@ -403,9 +419,9 @@
                 values = jnp.where(mine, value, jnp.ones_like(value))
                 queries = jnp.where(mine, query, tag_query)
                 blocks = []
-                for b in range(3):
+                for b in range(2):
                     scores = lax.dot_general(
-                        queries[b * 256 : (b + 1) * 256],
+                        queries[b * 384 : (b + 1) * 384],
                         keys,
                         (((1,), (1,)), ((), ())),
                         preferred_element_type=F32,
@@ -414,11 +430,11 @@
                     shifted = jnp.exp2((scores - highest) * EXP_SCALE).astype(BF16)
                     blocks.append(dot(shifted, values))
                 results.append(blocks)
-            for b in range(3):
-                half = low[:256]
+            for b in range(2):
+                half = low[:384]
                 top = jnp.where(half, results[0][b], results[1][b])
                 sums = jnp.where(half, results[1][b], results[0][b])
-                heads[which * 2 + p, b * 256 : (b + 1) * 256, :] = top / pltpu.roll(sums, 64, 1)
+                heads[which * 2 + p, b * 384 : (b + 1) * 384, :] = top / pltpu.roll(sums, 64, 1)
             for now in range(8):
                 at_step(step * 2 + p, now, *schedule[now])
             return carry
@@ -427,13 +443,13 @@
         return carry
 
     schedule = (
-        [(near, 3), (onward, 2, 0)],
-        [(onward, 2, 1), (onward, 2, 2)],
-        [(far, 3), (share, 2, 0), (share, 2, 1)],
-        [(share, 2, 2), (onward, 3, 0)],
-        [(onward, 3, 1)],
-        [(onward, 3, 2), (share, 3, 0)],
-        [(share, 3, 1)],
+        [(near, 1), (near, 2), (begin, 3)],
+        [(far, 1), (far, 2)],
+        [(onward, 1, 0), (onward, 1, 1), (onward, 1, 2), (onward, 2, 0)],
+        [(onward, 2, 1), (near, 3)],
+        [(onward, 2, 2), (share, 1, 0), (share, 1, 1), (share, 1, 2), (far, 3)],
+        [(share, 2, 0), (share, 2, 1), (share, 2, 2)],
+        [(share, 3, 0), (share, 3, 1)],
         [(share, 3, 2)],
     )
     lax.fori_loop(0, 4, attend, 0)
@@ -491,27 +507,27 @@
             at_step(step, i + 1, (ready, 2, i), (ready, 3, i))
 
         def widen(n, carry):
-            at = pl.multiple_of(n * 256, 256)
-            up = dot(normed[0:ROWS, :], w_up[which, :, pl.ds(at, 256)])
-            normed[ROWS:SLOTS, pl.ds(at, 256)] = jax.nn.gelu(up).astype(BF16)
+            at = pl.multiple_of(n * 1024, 1024)
+            up = dot(normed[0:ROWS, :], w_up[which, :, pl.ds(at, 1024)])
+            normed[ROWS:SLOTS, pl.ds(at, 1024)] = jax.nn.gelu(up).astype(BF16)
             return carry
 
-        lax.fori_loop(0, 4, widen, 0)
+        lax.fori_loop(0, 1, widen, 0)
 
         def narrow(n, carry):
-            at = pl.multiple_of(n * 256, 256)
-            total[:, pl.ds(at, 256)] = total[:, pl.ds(at, 256)] + dot(
-                normed[ROWS:SLOTS, :], w_down[which, :, pl.ds(at, 256)]
+            at = pl.multiple_of(n * 1024, 1024)
+            total[:, pl.ds(at, 1024)] = total[:, pl.ds(at, 1024)] + dot(
+                normed[ROWS:SLOTS, :], w_down[which, :, pl.ds(at, 1024)]
             )
             return carry
 
-        lax.fori_loop(0, 4, narrow, 0)
+        lax.fori_loop(0, 1, narrow, 0)
         return carry
 
     lax.fori_loop(0, 4, mlp, 0)
     out_ref[...] = total[...].astype(BF16)
     for w in range(4):
-        for slot in range(PER_WEIGHT):
+        for slot in slots_of(w):
             copy_of(w, slot).wait_send()
 
 

time: 136 us -> 123 us (0.904)
  Pallas kernels: 133 us -> 121 us
    pallas_call x1, Pallas kernels: 133 us -> 121 us  [local(): pl.pallas_call(kernel, out_shape=jax.ShapeDtypeStruct((ROWS, D), BF16), i...]
where the time goes in v3:
time: 123 us
  Pallas kernels  121 us (98%)
  local copies, waits for them, and re-layouts  2.06 us (2%)
    pallas_call x1, Pallas kernels, local(): pl.pallas_call(kernel, out_shape=jax.ShapeDtypeStruct((ROWS, D), BF16), i...  121 us

profile of v3, /device:TPU:1, one launch (start us, length us, event | category | flops | bytes accessed | tf_op | source)
XLA Modules:
  0.0 122.7 jit_solution(8387884848266943607)
XLA Ops:
  0.0 120.6 %shard_map.109 = bf16[384,1024]{1,0:T(8,128)(2,1)} custom-call(bf16[11,384,256]{2,1,0:T(8,128)(2,1)} %bitcast.3, bf16[11,256,1024]{2,1,0:T(8,128)(2,1)} %embed_ref.1, s32[384]{0:T(512)} %route_ref.1, s32[384]{0:T(512)} %frame_ref.1, s32[384]{0:T(512)} %fields_ref.1, f32[1,1024]{1,0:T(1,128)} %bitcast.4, f32[1,1024]{1,0:T(1,128)} %bitcast.5, ...), custom_call_target="tpu_custom_call" | custom-call | flops 24999999488 | bytes 16000000 | tf_op jit(solution)/shard_map/pallas_call | solution.py:540
  120.6 2.1 %copy.13 = bf16[384,1024]{1,0:T(8,128)(2,1)} copy(bf16[384,1024]{1,0:T(8,128)(2,1)} %shard_map.109) | data formatting | bytes 1572864

commit v4 on v3

--- a/solution.py
+++ b/solution.py
@@ -69,7 +69,6 @@
     rows,
     normed,
     qkv,
-    heads,
     hidden,
     total,
     gather,
@@ -434,7 +433,12 @@
                 half = low[:384]
                 top = jnp.where(half, results[0][b], results[1][b])
                 sums = jnp.where(half, results[1][b], results[0][b])
-                heads[which * 2 + p, b * 384 : (b + 1) * 384, :] = top / pltpu.roll(sums, 64, 1)
+                result = top / pltpu.roll(sums, 64, 1)
+                for k in range(3):
+                    first = (b * 3 + k) * CHUNKS + which * 2 + p
+                    stage[pl.ds(first, OWNERS, stride=NB_BACK), :] = result[
+                        k * OWNERS : (k + 1) * OWNERS
+                    ]
             for now in range(8):
                 at_step(step * 2 + p, now, *schedule[now])
             return carry
@@ -453,12 +457,6 @@
         [(share, 3, 2)],
     )
     lax.fori_loop(0, 4, attend, 0)
-
-    for k in range(MOST):
-        for n in range(CHUNKS):
-            stage[pl.ds(k * CHUNKS + n, OWNERS, stride=NB_BACK), :] = heads[
-                n, k * OWNERS : (k + 1) * OWNERS, :
-            ]
 
     def pack_back(k, carry):
         at = pl.multiple_of(k * 8 * NB_BACK, 8 * NB_BACK)
@@ -559,7 +557,6 @@
             pltpu.VMEM((SLOTS, D), F32),
             pltpu.VMEM((SLOTS, D), BF16),
             pltpu.VMEM((SLOTS, 768), BF16),
-            pltpu.VMEM((CHUNKS, SLOTS, 128), F32),
             pltpu.VMEM((ROWS, D), F32),
             pltpu.VMEM((ROWS, D), F32),
             pltpu.VMEM((ROWS, SLOTS), BF16),

time: 123 us -> 121 us (0.984)
  Pallas kernels: 121 us -> 119 us
    pallas_call x1, Pallas kernels: 121 us -> 119 us  [local(): pl.pallas_call(kernel, out_shape=jax.ShapeDtypeStruct((ROWS, D), BF16), i...]
where the time goes in v4:
time: 121 us
  Pallas kernels  119 us (98%)
  local copies, waits for them, and re-layouts  2.06 us (2%)
    pallas_call x1, Pallas kernels, local(): pl.pallas_call(kernel, out_shape=jax.ShapeDtypeStruct((ROWS, D), BF16), i...  119 us

profile of v4, /device:TPU:1, one launch (start us, length us, event | category | flops | bytes accessed | tf_op | source)
XLA Modules:
  0.0 121.3 jit_solution(7073816493587764865)
XLA Ops:
  0.0 119.2 %shard_map.109 = bf16[384,1024]{1,0:T(8,128)(2,1)} custom-call(bf16[11,384,256]{2,1,0:T(8,128)(2,1)} %bitcast.3, bf16[11,256,1024]{2,1,0:T(8,128)(2,1)} %embed_ref.1, s32[384]{0:T(512)} %route_ref.1, s32[384]{0:T(512)} %frame_ref.1, s32[384]{0:T(512)} %fields_ref.1, f32[1,1024]{1,0:T(1,128)} %bitcast.4, f32[1,1024]{1,0:T(1,128)} %bitcast.5, ...), custom_call_target="tpu_custom_call" | custom-call | flops 24999999488 | bytes 16000000 | tf_op jit(solution)/shard_map/pallas_call | solution.py:538
  119.2 2.1 %copy.13 = bf16[384,1024]{1,0:T(8,128)(2,1)} copy(bf16[384,1024]{1,0:T(8,128)(2,1)} %shard_map.109) | data formatting | bytes 1572864

commit v5 on v4

--- a/solution.py
+++ b/solution.py
@@ -451,10 +451,10 @@
         [(far, 1), (far, 2)],
         [(onward, 1, 0), (onward, 1, 1), (onward, 1, 2), (onward, 2, 0)],
         [(onward, 2, 1), (near, 3)],
-        [(onward, 2, 2), (share, 1, 0), (share, 1, 1), (share, 1, 2), (far, 3)],
+        [(onward, 2, 2), (share, 1, 0), (share, 1, 1), (share, 1, 2)],
+        [(far, 3)],
         [(share, 2, 0), (share, 2, 1), (share, 2, 2)],
-        [(share, 3, 0), (share, 3, 1)],
-        [(share, 3, 2)],
+        [],
     )
     lax.fori_loop(0, 4, attend, 0)
 
@@ -466,6 +466,8 @@
 
     lax.fori_loop(0, OWNERS // 8, pack_back, 0)
     own_back = exchange(send_back, recv_back, sems_back)
+    for i in range(3):
+        share(3, i)
     for i in range(3):
         ready(1, i)
     finish(send_back, recv_back, sems_back, own_back)

time: 121 us -> 120 us (level)
  no operation moved by 1% of the time
where the time goes in v5:
time: 120 us
  Pallas kernels  118 us (98%)
  local copies, waits for them, and re-layouts  2.06 us (2%)
    pallas_call x1, Pallas kernels, local(): pl.pallas_call(kernel, out_shape=jax.ShapeDtypeStruct((ROWS, D), BF16), i...  118 us

profile of v5, /device:TPU:1, one launch (start us, length us, event | category | flops | bytes accessed | tf_op | source)
XLA Modules:
  0.0 120.1 jit_solution(8447203142458597836)
XLA Ops:
  0.0 118.1 %shard_map.109 = bf16[384,1024]{1,0:T(8,128)(2,1)} custom-call(bf16[11,384,256]{2,1,0:T(8,128)(2,1)} %bitcast.3, bf16[11,256,1024]{2,1,0:T(8,128)(2,1)} %embed_ref.1, s32[384]{0:T(512)} %route_ref.1, s32[384]{0:T(512)} %frame_ref.1, s32[384]{0:T(512)} %fields_ref.1, f32[1,1024]{1,0:T(1,128)} %bitcast.4, f32[1,1024]{1,0:T(1,128)} %bitcast.5, ...), custom_call_target="tpu_custom_call" | custom-call | flops 24999999488 | bytes 16000000 | tf_op jit(solution)/shard_map/pallas_call | solution.py:540
  118.1 2.1 %copy.13 = bf16[384,1024]{1,0:T(8,128)(2,1)} copy(bf16[384,1024]{1,0:T(8,128)(2,1)} %shard_map.109) | data formatting | bytes 1572864
